TPU v7x, 32 devices: a whole 2x2x4 slice. The times are simulated.
32 devices in a mesh: groups: 2 (over y), blk: 8 (over z, x), heads: 2 (over core).
Axes of the slice: x: 2, y: 2, z: 4, core: 2. Of those that a mesh axis runs over, the one named last changes fastest.
Arguments:
- tokens: bfloat16 [6144, 1024], P(('groups', 'blk'), 'heads'), parts along dimension 0, may hold values from -96 to 96
- w_query: bfloat16 [1024, 1024], P(None, 'heads'), may hold values from -0.47851562 to 0.47851562
- w_key: bfloat16 [1024, 1024], P(None, 'heads'), may hold values from -0.1875 to 0.1875
- w_value: bfloat16 [1024, 1024], P(None, 'heads'), may hold values from -0.1875 to 0.1875
- hilbert_pos: int32 [6144], P(('groups', 'blk')), parts along dimension 0, may hold values from 0 to 3071, as said below
- key_blocks: int32 [48, 8], P(('groups', 'blk')), parts along dimension 0, may hold values from 0 to 23, as said below
- blend: int32 [6144], P(('groups', 'blk')), parts along dimension 0, may hold values from 1 to 8
Outputs:
- blended: bfloat16 [6144, 1024], P(('groups', 'blk'), 'heads'), parts along dimension 0
There are 2 independent parts, one for each index of `groups`. A program takes and returns all parts, laid end to end along the dimension named above; an argument that names none is the same for every part. Nothing has to cross between parts.
Inputs may be any that keep to these rules, and one draw needn't show every extreme that they name: `hilbert_pos`: A permutation of the 3072 positions. Each index of blk holds the sequence positions i * 384 to (i + 1) * 384 - 1; the 384 tile tokens of each index of blk go to every index exactly 48 at a time. `key_blocks`: row b names 8 distinct blocks, b itself among them. Block c lies on index c // 3 of blk; every listed block lies at most 2 indices from b's along the closed cycle of blk, and some row names blocks exactly 2 indices below and above its own.
All inputs are finite; a program needn't handle non-finite values.
Results may differ from a plain program's by a relative error of at most 0.0025.
The roundings to bfloat16 on the way count: a program that leaves them out, or rounds other values in their place, can miss the bound.
Values may be sent and summed in bfloat16 or wider, within the bound.
A program may use at most 64 MiB of HBM per device.

v0:
```python
import jax
import jax.numpy as jnp
from jax import lax
from jax.sharding import PartitionSpec as P

BLOCK = 128
LIST = 8
REACH = 2
BLEND = 8
HEAD_DIM = 64


def from_behind(value, axis, by):
    size = lax.axis_size(axis)
    return lax.ppermute(value, axis, [(i, (i + by) % size) for i in range(size)])


def project(rows_in, weight):
    return jnp.dot(rows_in, weight, preferred_element_type=jnp.float32).astype(jnp.bfloat16)


def join_heads(piece):
    return lax.all_gather(piece, "heads", axis=1, tiled=True)


def pass_along(paired, direction):
    return from_behind(paired, "blk", direction)


def shards(tokens, w_query, w_key, w_value, hilbert_pos, key_blocks, blend):
    cycle_len = lax.axis_size("blk")
    center = lax.axis_index("blk")
    rows = tokens.shape[0]
    per_peer = rows // cycle_len
    width = w_query.shape[1]
    blocks_dev = rows // BLOCK
    order = jnp.argsort(hilbert_pos)
    sent_pos = hilbert_pos[order].reshape(cycle_len, per_peer)
    moved, got_pos = (
        lax.all_to_all(
            tokens[order].reshape(cycle_len, per_peer, tokens.shape[1]),
            "blk",
            split_axis=0,
            concat_axis=0,
            tiled=True,
        ),
        lax.all_to_all(sent_pos, "blk", split_axis=0, concat_axis=0, tiled=True),
    )
    local = got_pos.reshape(rows) - center * rows
    placed = (
        jnp.zeros((rows, tokens.shape[1]), jnp.bfloat16)
        .at[local]
        .set(moved.reshape(rows, tokens.shape[1]))
    )
    full = join_heads(placed)
    query = project(full, w_query)
    keys = project(full, w_key)
    values = project(full, w_value)
    paired = jnp.stack([keys, values], 0)
    lower = []
    cursor = paired
    for step in range(REACH):
        cursor = pass_along(cursor, 1)
        lower.append(cursor)
    upper = []
    cursor = paired
    for step in range(REACH):
        cursor = pass_along(cursor, -1)
        upper.append(cursor)
    pieces = lower[::-1] + [paired] + upper
    window = jnp.concatenate(pieces, 1)
    span = (2 * REACH + 1) * blocks_dev
    window_keys = window[0].reshape(span, BLOCK, width)
    window_values = window[1].reshape(span, BLOCK, width)
    heads_here = width // HEAD_DIM

    def one_block(item):
        query_block, listed = item
        owner = listed // blocks_dev
        slot = (owner - center + REACH) % cycle_len * blocks_dev + listed % blocks_dev
        near_keys = window_keys[slot].reshape(LIST * BLOCK, heads_here, HEAD_DIM)
        near_values = window_values[slot].reshape(LIST * BLOCK, heads_here, HEAD_DIM)
        scores = jnp.einsum(
            "qhd,khd->hqk",
            query_block.reshape(BLOCK, heads_here, HEAD_DIM),
            near_keys,
            preferred_element_type=jnp.float32,
        ) * HEAD_DIM ** (-0.5)
        top = jnp.max(scores, axis=2, keepdims=True)
        weights = jnp.exp(scores - top)
        total = jnp.sum(weights, axis=2)
        mixed = jnp.einsum(
            "hqk,khd->qhd",
            weights.astype(jnp.bfloat16),
            near_values,
            preferred_element_type=jnp.float32,
        )
        return (mixed / jnp.transpose(total)[:, :, None]).astype(jnp.bfloat16).reshape(BLOCK, width)

    attended = lax.map(one_block, (query.reshape(blocks_dev, BLOCK, width), key_blocks)).reshape(
        rows, width
    )
    back = lax.all_to_all(
        attended[local].reshape(cycle_len, per_peer, width),
        "blk",
        split_axis=0,
        concat_axis=0,
        tiled=True,
    )
    restored = jnp.zeros((rows, width), jnp.bfloat16).at[order].set(back.reshape(rows, width))
    return (restored.astype(jnp.float32) * blend.astype(jnp.float32)[:, None] / BLEND).astype(
        jnp.bfloat16
    )


def solution(mesh):
    placed = (
        P(("groups", "blk"), "heads"),
        P(None, "heads"),
        P(None, "heads"),
        P(None, "heads"),
        P(("groups", "blk")),
        P(("groups", "blk"), None),
        P(("groups", "blk")),
    )
    return jax.shard_map(
        shards, mesh=mesh, in_specs=placed, out_specs=P(("groups", "blk"), "heads"), check_vma=False
    )
```

profile of v0, /device:TPU:0, one launch (start us, length us, event | category | flops | bytes accessed | tf_op | source)
XLA Modules:
  0.0 187.5 jit_solution(1796468157205685877)
XLA Ops:
  0.0 4.6 %sort.17 = (s32[384]{0:T(512)}, s32[384]{0:T(512)S(1)}) sort(s32[384]{0:T(512)} %param.13, s32[384]{0:T(512)S(1)} %iota.4), dimensions={0}, to_apply=%region_0.0 | sort | flops 3456 | bytes 6144 | tf_op jit(solution)/shard_map/jit(argsort)/sort | solution.py:37
  5.2 3.6 %gather_fusion.2 = s32[384]{0:T(512)S(1)} fusion(s32[384]{0:T(512)} %param.13, s32[1024]{0:T(1024)S(1)} %pad_clamp_fusion.2), kind=kCustom, calls=%fused_computation.2 | custom fusion | bytes 4608 | tf_op jit(solution)/shard_map/gather | solution.py:38
  9.5 7.3 %all-to-all-start = ((s32[8,1,48]{2,1,0:T(1,128)}), s32[8,1,48]{2,1,0:T(1,128)S(1)}, u32[]{:S(2)}, u32[]{:S(2)}) async-start(s32[8,1,48]{2,1,0:T(1,128)} %all_to_all.12), calls=%async_computation | async-start | bytes 8192 | tf_op jit(solution)/shard_map/all_to_all | solution.py:47
  16.7 2.6 %gather_fusion.3 = bf16[384,512]{1,0:T(8,128)(2,1)} fusion(bf16[384,512]{1,0:T(8,128)(2,1)S(1)} %copy-done.2, s32[1024]{0:T(1024)S(1)} %pad_clamp_fusion.2), kind=kCustom, calls=%fused_computation.3 | custom fusion | bytes 787968 | tf_op jit(solution)/shard_map/gather | solution.py:41
  19.3 3.9 %all-to-all-done = s32[8,1,48]{2,1,0:T(1,128)S(1)} async-done(((s32[8,1,48]{2,1,0:T(1,128)}), s32[8,1,48]{2,1,0:T(1,128)S(1)}, u32[]{:S(2)}, u32[]{:S(2)}) %all-to-all-start) | async-done | bytes 1568 | tf_op jit(solution)/shard_map/all_to_all | solution.py:47
  23.2 3.5 %all-to-all-start.1 = ((bf16[8,48,512]{2,1,0:T(8,128)(2,1)}), bf16[8,48,512]{2,1,0:T(8,128)(2,1)S(1)}, u32[]{:S(2)}, u32[]{:S(2)}) async-start(bf16[8,48,512]{2,1,0:T(8,128)(2,1)} %bitcast.8), calls=%async_computation.1 | async-start | bytes 786432 | tf_op jit(solution)/shard_map/all_to_all | solution.py:40
  26.8 10.3 %all-to-all-done.1 = bf16[8,48,512]{2,1,0:T(8,128)(2,1)S(1)} async-done(((bf16[8,48,512]{2,1,0:T(8,128)(2,1)}), bf16[8,48,512]{2,1,0:T(8,128)(2,1)S(1)}, u32[]{:S(2)}, u32[]{:S(2)}) %all-to-all-start.1) | async-done | bytes 393248 | tf_op jit(solution)/shard_map/all_to_all | solution.py:40
  39.1 2.4 %all_gather.3 = bf16[384,1024]{1,0:T(8,128)(2,1)S(1)} all-gather(bf16[384,512]{1,0:T(8,128)(2,1)S(1)} %scatter_custom_fusion), channel_id=1, replica_groups=mesh['groups'=2,'blk'=8,'heads'=2] {'heads'}, dimensions={1}, use_global_device_ids=true | all-gather | bytes 1179648 | tf_op jit(solution)/shard_map/all_gather | solution.py:23
  45.1 3.3 %collective-permute-start.2 = (bf16[2,384,512]{2,1,0:T(8,128)(2,1)}, bf16[2,384,512]{2,1,0:T(8,128)(2,1)S(1)}, u32[]{:S(2)}, u32[]{:S(2)}) collective-permute-start(bf16[2,384,512]{2,1,0:T(8,128)(2,1)} %pad_maximum_fusion), channel_id=1, source_target_pairs={{0,14},{2,0},{4,2},{6,4},{8,6},{10,8},{12,10},{14,12},{1,15},{3,1}... | collective-permute-start | bytes 2359304 | tf_op jit(solution)/shard_map/ppermute | solution.py:15
  48.4 31.0 %collective-permute-done = bf16[2,384,512]{2,1,0:T(8,128)(2,1)} collective-permute-done((bf16[2,384,512]{2,1,0:T(8,128)(2,1)}, bf16[2,384,512]{2,1,0:T(8,128)(2,1)}, u32[]{:S(2)}, u32[]{:S(2)}) %collective-permute-start) | collective-permute-done | bytes 786464 | tf_op jit(solution)/shard_map/ppermute | solution.py:15
  79.4 2.5 %collective-permute-start.1 = (bf16[2,384,512]{2,1,0:T(8,128)(2,1)}, bf16[2,384,512]{2,1,0:T(8,128)(2,1)}, u32[]{:S(2)}, u32[]{:S(2)}) collective-permute-start(bf16[2,384,512]{2,1,0:T(8,128)(2,1)} %collective-permute-done), channel_id=1, source_target_pairs={{0,2},{2,4},{4,6},{6,8},{8,10},{10,12},{12,14},{14,0},{1,3},{3,5},... | collective-permute-start | bytes 2359304 | tf_op jit(solution)/shard_map/ppermute | solution.py:15
  81.9 2.3 %collective-permute-start.3 = (bf16[2,384,512]{2,1,0:T(8,128)(2,1)S(1)}, bf16[2,384,512]{2,1,0:T(8,128)(2,1)S(1)}, u32[]{:S(2)}, u32[]{:S(2)}) collective-permute-start(bf16[2,384,512]{2,1,0:T(8,128)(2,1)S(1)} %collective-permute-done.2), channel_id=1, source_target_pairs={{0,14},{2,0},{4,2},{6,4},{8,6},{10,8},{12,10},{14,12},{1,15},{3,1}... | collective-permute-start | bytes 2359304 | tf_op jit(solution)/shard_map/ppermute | solution.py:15
  84.2 2.8 %convolution_convert_fusion = bf16[384,512]{1,0:T(8,128)(2,1)} fusion(bf16[384,1024]{1,0:T(8,128)(2,1)} %copy-done.3, bf16[1024,512]{1,0:T(8,128)(2,1)} %param.10), kind=kOutput, calls=%fused_computation.33 | convolution fusion | flops 402849792 | bytes 2228224 | tf_op jit(solution)/shard_map/dot_general | solution.py:19
  87.0 28.3 %collective-permute-done.1 = bf16[2,384,512]{2,1,0:T(8,128)(2,1)} collective-permute-done((bf16[2,384,512]{2,1,0:T(8,128)(2,1)}, bf16[2,384,512]{2,1,0:T(8,128)(2,1)}, u32[]{:S(2)}, u32[]{:S(2)}) %collective-permute-start.1) | collective-permute-done | bytes 786464 | tf_op jit(solution)/shard_map/ppermute | solution.py:15
  120.0 46.9 %while.13 = (s32[]{:T(128)}, bf16[3,128,512]{2,1,0:T(8,128)(2,1)S(1)}, s32[3,8]{1,0:T(4,128)}, s32[]{:T(128)}, bf16[15,128,512]{2,1,0:T(8,128)(2,1)}, /*index=5*...) while((s32[]{:T(128)}, bf16[3,128,512]{2,1,0:T(8,128)(2,1)S(1)}, s32[3,8]{1,0:T(4,128)}, ...), condition=%wide.region_5.6_spmd, body=%wide.region_2.5_spmd.sunk | while | flops 276954368 | bytes 45375776 | solution.py:100
  120.7 2.2 %gather_fusion.1 = bf16[8,128,512]{2,1,0:T(8,128)(2,1)S(1)} fusion(bf16[15,128,512]{2,1,0:T(8,128)(2,1)} %get-tuple-element.230, s32[1024]{0:T(1024)S(1)} %pad_clamp_fusion.4), kind=kCustom, calls=%fused_computation.1.clone.1 | custom fusion | bytes 2097184 | tf_op jit(solution)/shard_map/while/body/eval_jaxpr/gather | solution.py:81
  132.3 3.1 %fusion.51 = bf16[128,8,64]{0,2,1:T(8,128)(2,1)S(1)} fusion(bf16[1024,8,64]{0,2,1:T(8,128)(2,1)S(1)} %reshape.286, f32[8,128,1024]{2,1,0:T(8,128)} %copy-done.1, f32[8,128]{1,0:T(8,128)S(1)} %get-tuple-element.207, f32[128,8]{0,1:T(8,128)S(1)} %bitcast.87), kind=kOutput, calls=%fused_computation.16.clone.1 | convolution fusion | flops 137494528 | bytes 5382144 | tf_op jit(solution)/shard_map/while/body/eval_jaxpr/hqk,khd->qhd/dot_general | solution.py:92
  147.9 3.1 %fusion.51 = bf16[128,8,64]{0,2,1:T(8,128)(2,1)S(1)} fusion(bf16[1024,8,64]{0,2,1:T(8,128)(2,1)S(1)} %reshape.286, f32[8,128,1024]{2,1,0:T(8,128)} %copy-done.1, f32[8,128]{1,0:T(8,128)S(1)} %get-tuple-element.207, f32[128,8]{0,1:T(8,128)S(1)} %bitcast.87), kind=kOutput, calls=%fused_computation.16.clone.1 | convolution fusion | flops 137494528 | bytes 5382144 | tf_op jit(solution)/shard_map/while/body/eval_jaxpr/hqk,khd->qhd/dot_general | solution.py:92
  152.0 2.2 %gather_fusion.1 = bf16[8,128,512]{2,1,0:T(8,128)(2,1)S(1)} fusion(bf16[15,128,512]{2,1,0:T(8,128)(2,1)} %get-tuple-element.230, s32[1024]{0:T(1024)S(1)} %pad_clamp_fusion.4), kind=kCustom, calls=%fused_computation.1.clone.1 | custom fusion | bytes 2097184 | tf_op jit(solution)/shard_map/while/body/eval_jaxpr/gather | solution.py:81
  163.6 3.1 %fusion.51 = bf16[128,8,64]{0,2,1:T(8,128)(2,1)S(1)} fusion(bf16[1024,8,64]{0,2,1:T(8,128)(2,1)S(1)} %reshape.286, f32[8,128,1024]{2,1,0:T(8,128)} %copy-done.1, f32[8,128]{1,0:T(8,128)S(1)} %get-tuple-element.207, f32[128,8]{0,1:T(8,128)S(1)} %bitcast.87), kind=kOutput, calls=%fused_computation.16.clone.1 | convolution fusion | flops 137494528 | bytes 5382144 | tf_op jit(solution)/shard_map/while/body/eval_jaxpr/hqk,khd->qhd/dot_general | solution.py:92
  166.9 2.6 %gather_fusion.4 = bf16[384,512]{1,0:T(8,128)(2,1)} fusion(bf16[384,512]{1,0:T(8,128)(2,1)S(1)} %bitcast.81, s32[1024]{0:T(1024)S(1)} %pad_clamp_fusion.1), kind=kCustom, calls=%fused_computation.4 | custom fusion | bytes 787968 | tf_op jit(solution)/shard_map/gather | solution.py:104
  169.5 4.7 %all-to-all-start.2 = ((bf16[8,48,512]{2,1,0:T(8,128)(2,1)}), bf16[8,48,512]{2,1,0:T(8,128)(2,1)S(1)}, u32[]{:S(2)}, u32[]{:S(2)}) async-start(bf16[8,48,512]{2,1,0:T(8,128)(2,1)} %bitcast.16), calls=%async_computation.2 | async-start | bytes 786432 | tf_op jit(solution)/shard_map/all_to_all | solution.py:103
  174.2 10.2 %all-to-all-done.2 = bf16[8,48,512]{2,1,0:T(8,128)(2,1)S(1)} async-done(((bf16[8,48,512]{2,1,0:T(8,128)(2,1)}), bf16[8,48,512]{2,1,0:T(8,128)(2,1)S(1)}, u32[]{:S(2)}, u32[]{:S(2)}) %all-to-all-start.2) | async-done | bytes 393248 | tf_op jit(solution)/shard_map/all_to_all | solution.py:103
  184.4 2.2 %scatter_custom_fusion.1 = bf16[384,512]{1,0:T(8,128)(2,1)S(1)} fusion(s32[384]{0:T(512)} %copy-done.4, bf16[384,512]{1,0:T(8,128)(2,1)S(1)} %bitcast.86, bf16[]{:T(256)} %constant.107.clone.1), kind=kCustom, calls=%fused_computation.40 | custom fusion | bytes 393728 | tf_op jit(solution)/shard_map/scatter | solution.py:110
  (82 shorter events, 45.4 us)
Async XLA Ops:
  0.0 41.5 %copy-start = (bf16[1024,512]{1,0:T(8,128)(2,1)S(1)}, bf16[1024,512]{1,0:T(8,128)(2,1)}, u32[]{:S(2)}) copy-start(bf16[1024,512]{1,0:T(8,128)(2,1)} %param.11) | copy-start | bytes 3145732
  0.0 16.7 %copy-start.2 = (bf16[384,512]{1,0:T(8,128)(2,1)S(1)}, bf16[384,512]{1,0:T(8,128)(2,1)}, u32[]{:S(2)}) copy-start(bf16[384,512]{1,0:T(8,128)(2,1)} %param.9) | copy-start | bytes 1179652
  4.6 0.6 copy-start.4
  9.5 13.7 %all-to-all-start = ((s32[8,1,48]{2,1,0:T(1,128)}), s32[8,1,48]{2,1,0:T(1,128)S(1)}, u32[]{:S(2)}, u32[]{:S(2)}) async-start(s32[8,1,48]{2,1,0:T(1,128)} %all_to_all.12), calls=%async_computation | async-start | bytes 8192 | tf_op jit(solution)/shard_map/all_to_all | solution.py:47
  16.7 25.4 %copy-start.6 = (bf16[1024,512]{1,0:T(8,128)(2,1)S(1)}, bf16[1024,512]{1,0:T(8,128)(2,1)}, u32[]{:S(2)}) copy-start(bf16[1024,512]{1,0:T(8,128)(2,1)} %param.12) | copy-start | bytes 3145732
  23.2 13.9 %all-to-all-start.1 = ((bf16[8,48,512]{2,1,0:T(8,128)(2,1)}), bf16[8,48,512]{2,1,0:T(8,128)(2,1)S(1)}, u32[]{:S(2)}, u32[]{:S(2)}) async-start(bf16[8,48,512]{2,1,0:T(8,128)(2,1)} %bitcast.8), calls=%async_computation.1 | async-start | bytes 786432 | tf_op jit(solution)/shard_map/all_to_all | solution.py:40
  41.5 37.9 %copy-start.3 = (bf16[384,1024]{1,0:T(8,128)(2,1)}, bf16[384,1024]{1,0:T(8,128)(2,1)S(1)}, u32[]{:S(2)}) copy-start(bf16[384,1024]{1,0:T(8,128)(2,1)S(1)} %all_gather.3) | copy-start | bytes 2359300
  43.6 35.7 %collective-permute-start = (bf16[2,384,512]{2,1,0:T(8,128)(2,1)}, bf16[2,384,512]{2,1,0:T(8,128)(2,1)}, u32[]{:S(2)}, u32[]{:S(2)}) collective-permute-start(bf16[2,384,512]{2,1,0:T(8,128)(2,1)} %pad_maximum_fusion), channel_id=1, source_target_pairs={{0,2},{2,4},{4,6},{6,8},{8,10},{10,12},{12,14},{14,0},{1,3},{3,5},... | collective-permute-start | bytes 2359304 | tf_op jit(solution)/shard_map/ppermute | solution.py:15
  45.1 36.8 %collective-permute-start.2 = (bf16[2,384,512]{2,1,0:T(8,128)(2,1)}, bf16[2,384,512]{2,1,0:T(8,128)(2,1)S(1)}, u32[]{:S(2)}, u32[]{:S(2)}) collective-permute-start(bf16[2,384,512]{2,1,0:T(8,128)(2,1)} %pad_maximum_fusion), channel_id=1, source_target_pairs={{0,14},{2,0},{4,2},{6,4},{8,6},{10,8},{12,10},{14,12},{1,15},{3,1}... | collective-permute-start | bytes 2359304 | tf_op jit(solution)/shard_map/ppermute | solution.py:15
  79.4 35.9 %collective-permute-start.1 = (bf16[2,384,512]{2,1,0:T(8,128)(2,1)}, bf16[2,384,512]{2,1,0:T(8,128)(2,1)}, u32[]{:S(2)}, u32[]{:S(2)}) collective-permute-start(bf16[2,384,512]{2,1,0:T(8,128)(2,1)} %collective-permute-done), channel_id=1, source_target_pairs={{0,2},{2,4},{4,6},{6,8},{8,10},{10,12},{12,14},{14,0},{1,3},{3,5},... | collective-permute-start | bytes 2359304 | tf_op jit(solution)/shard_map/ppermute | solution.py:15
  81.9 35.9 %collective-permute-start.3 = (bf16[2,384,512]{2,1,0:T(8,128)(2,1)S(1)}, bf16[2,384,512]{2,1,0:T(8,128)(2,1)S(1)}, u32[]{:S(2)}, u32[]{:S(2)}) collective-permute-start(bf16[2,384,512]{2,1,0:T(8,128)(2,1)S(1)} %collective-permute-done.2), channel_id=1, source_target_pairs={{0,14},{2,0},{4,2},{6,4},{8,6},{10,8},{12,10},{14,12},{1,15},{3,1}... | collective-permute-start | bytes 2359304 | tf_op jit(solution)/shard_map/ppermute | solution.py:15
  126.0 1.9 %copy-start.1 = (f32[8,128,1024]{2,1,0:T(8,128)}, f32[8,128,1024]{2,1,0:T(8,128)S(1)}, u32[]{:S(2)}) copy-start(f32[8,128,1024]{2,1,0:T(8,128)S(1)} %get-tuple-element.206) | copy-start | bytes 12582916 | tf_op jit(solution)/shard_map/while
  141.7 1.9 %copy-start.1 = (f32[8,128,1024]{2,1,0:T(8,128)}, f32[8,128,1024]{2,1,0:T(8,128)S(1)}, u32[]{:S(2)}) copy-start(f32[8,128,1024]{2,1,0:T(8,128)S(1)} %get-tuple-element.206) | copy-start | bytes 12582916 | tf_op jit(solution)/shard_map/while
  157.3 1.9 %copy-start.1 = (f32[8,128,1024]{2,1,0:T(8,128)}, f32[8,128,1024]{2,1,0:T(8,128)S(1)}, u32[]{:S(2)}) copy-start(f32[8,128,1024]{2,1,0:T(8,128)S(1)} %get-tuple-element.206) | copy-start | bytes 12582916 | tf_op jit(solution)/shard_map/while
  166.9 7.3 %copy-start.5 = (s32[384]{0:T(512)S(1)}, s32[384]{0:T(512)}, u32[]{:S(2)}) copy-start(s32[384]{0:T(512)} %param.15) | copy-start | bytes 4612
  169.5 14.9 %all-to-all-start.2 = ((bf16[8,48,512]{2,1,0:T(8,128)(2,1)}), bf16[8,48,512]{2,1,0:T(8,128)(2,1)S(1)}, u32[]{:S(2)}, u32[]{:S(2)}) async-start(bf16[8,48,512]{2,1,0:T(8,128)(2,1)} %bitcast.16), calls=%async_computation.2 | async-start | bytes 786432 | tf_op jit(solution)/shard_map/all_to_all | solution.py:103
where the time goes:
time: 188 us; the launch traced here: 187 us
  waiting for transfers between devices  83.8 us (45%)
  local copies, waits for them, and re-layouts  48.7 us (26%)
  starting transfers between devices  24.9 us (13%)
  matrix products  15.9 us (8%)
  other arithmetic  11.4 us (6%)
  blocking collectives  2.37 us (1%)
    ppermute x4, waiting for transfers between devices, from_behind(): lax.ppermute(value, axis, [(i, (i + by) % size) for i in range(size)])  59.4 us
    all_to_all x1, waiting for transfers between devices, shards(): lax.all_to_all(tokens[order].reshape(cycle_len, per_peer, tokens.shape[1]...  10.3 us
    all_to_all x1, waiting for transfers between devices, shards(): lax.all_to_all(attended[local].reshape(cycle_len, per_peer, width), 'blk'...  10.2 us
    ppermute x4, starting transfers between devices, from_behind(): lax.ppermute(value, axis, [(i, (i + by) % size) for i in range(size)])  9.5 us
    dot_general x3, matrix products, one_block(): jnp.einsum('hqk,khd->qhd', weights.astype(jnp.bfloat16), near_values, pre...  9.44 us
    gather x6, local copies, waits for them, and re-layouts, one_block(): near_keys = window_keys[slot].reshape(LIST * BLOCK, heads_here, HEAD_DIM)  8.74 us
    gather x6, local copies, waits for them, and re-layouts, one_block(): window_values[slot].reshape(LIST * BLOCK, heads_here, HEAD_DIM)  8.74 us
    all_to_all x1, starting transfers between devices, shards(): lax.all_to_all(sent_pos, 'blk', split_axis=0, concat_axis=0, tiled=True)  7.25 us
  transfers between devices with their start and end apart: 7, of which 5 were waited for; matrix products, arithmetic and copies ran while one was open for 4% of the time, Pallas kernels for 0%

commit v1 on v0

v1 whole, which is shorter than its diff:
```python
import functools

import jax
import jax.numpy as jnp
from jax import lax
from jax.experimental import pallas as pl
from jax.experimental.pallas import tpu as pltpu
from jax.sharding import PartitionSpec as P

BLOCK = 128
LIST = 8
REACH = 2
BLEND = 8
HEAD_DIM = 64
PIECES = 2
WINDOW = 2 * REACH + 1
LOG2_E = 1.4426950408889634
MESH = pl.DeviceIdType.MESH
F32 = jnp.float32
BF16 = jnp.bfloat16


def remote(src, dst, send_sem, recv_sem, where):
    return pltpu.make_async_remote_copy(
        src_ref=src,
        dst_ref=dst,
        send_sem=send_sem,
        recv_sem=recv_sem,
        device_id=where,
        device_id_type=MESH,
    )


def over_peers(n, body):
    if n <= 8:
        for k in range(1, n):
            body(k)
    else:
        lax.fori_loop(1, n, lambda k, c: (body(k), c)[1], 0)


def iota(shape, axis):
    return lax.broadcasted_iota(jnp.int32, shape, axis).astype(F32)


def contract(a, b, da, db):
    return lax.dot_general(a, b, (((da,), (db,)), ((), ())), preferred_element_type=F32)


def kernel(
    n, tok, pos, listed, wq, wk, wv, out,
    send, recv, code_out, code_in, spread, gather, win, qb, kb, vb, att, back_out, back_in, wq_v, wk_v, wv_v,
    w_sem, tok_s, tok_r, code_s, code_r, own_s, fwd_s, win_r, core_s, core_r, back_s, back_r,
):
    rows, width = tok.shape
    pp = send.shape[1]
    per_peer = rows // n
    nb = rows // BLOCK
    total_rows = n * pp
    me = lax.axis_index("blk")
    half = lax.axis_index("heads")
    e = 1 - 2 * lax.rem(me, 2)
    other = {"heads": 1 - half}

    def peer(k):
        return lax.rem(me + k + n, n)

    barrier = pltpu.get_barrier_semaphore()
    over_peers(n, lambda k: pl.semaphore_signal(barrier, inc=1, device_id={"blk": peer(k)}, device_id_type=MESH))
    pl.semaphore_signal(barrier, inc=1, device_id=other, device_id_type=MESH)

    loads = [
        pltpu.make_async_copy(src, dst, w_sem.at[i])
        for i, (src, dst) in enumerate(((wq, wq_v), (wk, wk_v), (wv, wv_v)))
    ]
    for load in loads:
        load.start()

    place = pos[...].astype(F32)
    column = jnp.sum(
        jnp.where(iota((rows, rows), 0) == iota((rows, rows), 1), place, 0.0), axis=1, keepdims=True
    )
    rank = jnp.sum(jnp.where(column < place, 1.0, 0.0), axis=0, keepdims=True)
    owner = jnp.sum(
        jnp.where(place >= (iota((n, rows), 0) + 1.0) * rows, 1.0, 0.0), axis=0, keepdims=True
    )
    slot_in = rank - owner * per_peer
    spread[...] = jnp.where(iota((total_rows, rows), 0) == owner * pp + slot_in, 1.0, 0.0).astype(BF16)
    code = place - owner * rows + 1.0
    high = jnp.floor(code * (1.0 / 128))
    low = code - high * 128
    mine = iota((n, rows), 0) == owner
    at = jnp.where(
        iota((total_rows, rows), 0) == slot_in + (me * pp).astype(F32), 1.0, 0.0
    ).astype(BF16)
    codes = 128.0 * contract(jnp.where(mine, high, 0.0).astype(BF16), at, 1, 1) + contract(
        jnp.where(mine, low, 0.0).astype(BF16), at, 1, 1
    )
    for d in range(n):
        code_out[d] = codes[d : d + 1, :]
    send[...] = contract(spread[...], tok[...], 1, 0).astype(BF16).reshape(n, pp, width)

    pl.semaphore_wait(barrier, n)

    def send_code(k):
        remote(code_out.at[peer(k)], code_in.at[me], code_s.at[k], code_r.at[k], {"blk": peer(k)}).start()

    def send_rows(k):
        remote(send.at[peer(k)], recv.at[me], tok_s.at[k], tok_r.at[k], {"blk": peer(k)}).start()

    over_peers(n, send_code)
    over_peers(n, send_rows)
    code_in[me] = code_out[me]
    recv[me] = send[me]

    def take_code(k):
        remote(code_out.at[peer(k)], code_in.at[peer(-k)], code_s.at[k], code_r.at[k], {"blk": peer(k)}).wait()

    def take_rows(k):
        remote(send.at[peer(k)], recv.at[peer(-k)], tok_s.at[k], tok_r.at[k], {"blk": peer(k)}).wait()

    over_peers(n, take_code)
    arrived = jnp.sum(code_in[...], axis=0)
    gather[...] = jnp.where(iota((rows, total_rows), 0) + 1.0 == arrived, 1.0, 0.0).astype(BF16)
    over_peers(n, take_rows)
    placed = contract(gather[...], recv[...].reshape(total_rows, width), 1, 0).astype(BF16)
    win[half, REACH] = placed

    def piece(step, c):
        return win.at[half, REACH + step, pl.ds(c * BLOCK, BLOCK)]

    def own_copy(i, step, c):
        return remote(
            piece(0, c), piece(-step, c), own_s.at[i, c], win_r.at[REACH - step, c], {"blk": peer(step)}
        )

    def fwd_copy(c):
        return remote(piece(2 * e, c), piece(e, c), fwd_s.at[c], win_r.at[REACH + e, c], {"blk": peer(e)})

    def core_copy(step, c):
        return remote(
            piece(step, c), piece(step, c), core_s.at[REACH + step, c], core_r.at[REACH + step, c], other
        )

    def arrival(step, c):
        return remote(piece(0, c), piece(step, c), own_s.at[0, c], win_r.at[REACH + step, c], {"blk": peer(step)})

    def core_arrival(step, c):
        return remote(
            piece(step, c),
            win.at[1 - half, REACH + step, pl.ds(c * BLOCK, BLOCK)],
            core_s.at[REACH + step, c],
            core_r.at[REACH + step, c],
            other,
        )

    steps_out = (-2 * e, 2 * e, e)
    for c in range(nb):
        for i, step in enumerate(steps_out):
            own_copy(i, step, c).start()
        core_copy(0, c).start()

    def project(step, with_query):
        for c in range(nb):
            core_arrival(step, c).wait_recv()
        slot = REACH + step
        whole = jnp.concatenate([win[0, slot], win[1, slot]], axis=1)
        if with_query:
            qb[...] = contract(whole, wq_v[...], 1, 0).astype(BF16).reshape(nb, BLOCK, width)
        kb[pl.ds(slot * nb, nb)] = contract(whole, wk_v[...], 1, 0).astype(BF16).reshape(nb, BLOCK, width)
        vb[pl.ds(slot * nb, nb)] = contract(whole, wv_v[...], 1, 0).astype(BF16).reshape(nb, BLOCK, width)

    def pass_on(step, forward):
        for c in range(nb):
            arrival(step, c).wait_recv()
            if forward:
                fwd_copy(c).start()
            core_copy(step, c).start()

    for load in loads:
        load.wait()
    project(0, True)
    pass_on(2 * e, True)
    pass_on(e, False)
    project(2 * e, False)
    project(e, False)
    pass_on(-2 * e, False)
    project(-2 * e, False)
    pass_on(-e, False)
    project(-e, False)

    first = lax.broadcasted_iota(jnp.int32, (BLOCK, 2 * HEAD_DIM), 1) < HEAD_DIM
    zero = jnp.zeros((BLOCK, 2 * HEAD_DIM), BF16)

    def attend(b, p, start):
        lanes = pl.ds(start, 2 * HEAD_DIM)
        slots = []
        for j in range(LIST):
            block = listed[b, j]
            away = jnp.minimum(lax.rem(lax.div(block, nb) - me + REACH + n, n), WINDOW - 1)
            slots.append(away * nb + lax.rem(block, nb))
        q = qb[b, :, lanes]
        both = jnp.concatenate([jnp.where(first, q, zero), jnp.where(first, zero, q)], axis=0)
        keys = jnp.concatenate([kb[s, :, lanes] for s in slots], axis=0)
        values = jnp.concatenate([vb[s, :, lanes] for s in slots], axis=0)
        scores = contract(both, keys, 1, 1)
        top = jnp.max(scores, axis=1, keepdims=True)
        weights = jnp.exp2((scores - top) * (HEAD_DIM ** (-0.5) * LOG2_E))
        total = jnp.sum(weights, axis=1, keepdims=True)
        mixed = contract(weights.astype(BF16), values, 1, 0) / total
        return jnp.where(first, mixed[:BLOCK], mixed[BLOCK:]).astype(BF16)

    part = width // PIECES
    pairs = part // (2 * HEAD_DIM)

    def back_copy(f, k, source):
        return remote(
            back_out.at[f, peer(k)], back_in.at[f, source], back_s.at[f, k], back_r.at[f, k], {"blk": peer(k)}
        )

    for f in range(PIECES):
        for p in range(pairs):

            @pl.loop(0, nb)
            def _(b):
                att[b, :, pl.ds(p * 2 * HEAD_DIM, 2 * HEAD_DIM)] = attend(b, p, f * part + p * 2 * HEAD_DIM)

        back_out[f] = (
            contract(gather[...], att[...].reshape(rows, part), 0, 0).astype(BF16).reshape(n, pp, part)
        )
        over_peers(n, lambda k: back_copy(f, k, me).start())
        back_in[f, me] = back_out[f, me]

    for c in range(nb):
        for i, step in enumerate(steps_out):
            own_copy(i, step, c).wait_send()
        fwd_copy(c).wait_send()
        for step in range(-REACH, REACH + 1):
            core_copy(step, c).wait_send()

    for f in range(PIECES):
        over_peers(n, lambda k: back_copy(f, k, peer(-k)).wait())
        out[:, pl.ds(f * part, part)] = contract(
            spread[...], back_in[f].reshape(total_rows, part), 0, 0
        ).astype(BF16)


def shards(n, tokens, w_query, w_key, w_value, hilbert_pos, key_blocks, blend):
    rows, width = tokens.shape
    depth = w_query.shape[0]
    per_peer = rows // n
    pp = -(-per_peer // 16) * 16
    nb = rows // BLOCK
    part = width // PIECES
    vmem = pl.BlockSpec(memory_space=pltpu.VMEM)
    anywhere = pl.BlockSpec(memory_space=pl.ANY)
    dma = pltpu.SemaphoreType.DMA
    restored = pl.pallas_call(
        functools.partial(kernel, n),
        out_shape=jax.ShapeDtypeStruct((rows, width), BF16),
        in_specs=[vmem, vmem, pl.BlockSpec(memory_space=pltpu.SMEM), anywhere, anywhere, anywhere],
        out_specs=vmem,
        scratch_shapes=[
            pltpu.VMEM((n, pp, width), BF16),
            pltpu.VMEM((n, pp, width), BF16),
            pltpu.VMEM((n, 1, n * pp), F32),
            pltpu.VMEM((n, 1, n * pp), F32),
            pltpu.VMEM((n * pp, rows), BF16),
            pltpu.VMEM((rows, n * pp), BF16),
            pltpu.VMEM((2, WINDOW, rows, width), BF16),
            pltpu.VMEM((nb, BLOCK, width), BF16),
            pltpu.VMEM((WINDOW * nb, BLOCK, width), BF16),
            pltpu.VMEM((WINDOW * nb, BLOCK, width), BF16),
            pltpu.VMEM((nb, BLOCK, part), BF16),
            pltpu.VMEM((PIECES, n, pp, part), BF16),
            pltpu.VMEM((PIECES, n, pp, part), BF16),
            pltpu.VMEM((depth, width), BF16),
            pltpu.VMEM((depth, width), BF16),
            pltpu.VMEM((depth, width), BF16),
            dma((3,)),
            dma((n,)),
            dma((n,)),
            dma((n,)),
            dma((n,)),
            dma((3, nb)),
            dma((nb,)),
            dma((WINDOW, nb)),
            dma((WINDOW, nb)),
            dma((WINDOW, nb)),
            dma((PIECES, n)),
            dma((PIECES, n)),
        ],
        compiler_params=pltpu.CompilerParams(
            collective_id=0, has_side_effects=True, vmem_limit_bytes=56 * 1024 * 1024
        ),
    )(tokens, hilbert_pos.reshape(1, rows), key_blocks, w_query, w_key, w_value)
    return (restored.astype(F32) * blend.astype(F32)[:, None] / BLEND).astype(BF16)


def solution(mesh):
    placed = (
        P(("groups", "blk"), "heads"),
        P(None, "heads"),
        P(None, "heads"),
        P(None, "heads"),
        P(("groups", "blk")),
        P(("groups", "blk"), None),
        P(("groups", "blk")),
    )
    return jax.shard_map(
        functools.partial(shards, mesh.shape["blk"]),
        mesh=mesh,
        in_specs=placed,
        out_specs=P(("groups", "blk"), "heads"),
        check_vma=False,
    )
```

time: 188 us -> 61.1 us (0.33)
  waiting for transfers between devices: 83.8 us -> 0 us
  Pallas kernels: 0 us -> 57.8 us
  local copies, waits for them, and re-layouts: 48.7 us -> 1.25 us
  starting transfers between devices: 24.9 us -> 0 us
  matrix products: 15.9 us -> 0 us
  other arithmetic: 11.4 us -> 1.91 us
  blocking collectives: 2.37 us -> 0 us
    ppermute x4 -> x0, waiting for transfers between devices: 59.4 us -> none  [from_behind(): lax.ppermute(value, axis, [(i, (i + by) % size) for i in range(size)])]
    pallas_call x0 -> x1, Pallas kernels: none -> 57.8 us  [shards(): pl.pallas_call(functools.partial(kernel, n), out_shape=jax.ShapeDtypeStru...]
    gather x15 -> x0, local copies, waits for them, and re-layouts: 26.3 us -> none  [the longest x6 8.74 us: one_block(): near_keys = window_keys[slot].reshape(LIST * BLOCK, heads_here, HEAD_DIM)]
    all_to_all x3 -> x0, waiting for transfers between devices: 24.4 us -> none  [the longest x1 10.3 us: shards(): lax.all_to_all(tokens[order].reshape(cycle_len, per_peer, tokens.shape[1]...]
    dot_general x9 -> x0, matrix products: 15.9 us -> none  [the longest x3 9.44 us: one_block(): jnp.einsum('hqk,khd->qhd', weights.astype(jnp.bfloat16), near_values, pre...]
    all_to_all x3 -> x0, starting transfers between devices: 15.4 us -> none  [the longest x1 7.25 us: shards(): lax.all_to_all(sent_pos, 'blk', split_axis=0, concat_axis=0, tiled=True)]
    ppermute x4 -> x0, starting transfers between devices: 9.5 us -> none  [from_behind(): lax.ppermute(value, axis, [(i, (i + by) % size) for i in range(size)])]
    while x6 -> x0, local copies, waits for them, and re-layouts: 5.77 us -> none
  transfers between devices with their start and end apart: 7 -> 0, of which waited for: 5 -> 0; matrix products, arithmetic and copies ran while one was open for 4% -> 0% of each run, Pallas kernels for 0% -> 0%
where the time goes in v1:
time: 61.1 us; the launch traced here: 60.9 us
  Pallas kernels  57.8 us (95%)
  other arithmetic  1.91 us (3%)
  local copies, waits for them, and re-layouts  1.25 us (2%)
    pallas_call x1, Pallas kernels, shards(): pl.pallas_call(functools.partial(kernel, n), out_shape=jax.ShapeDtypeStru...  57.8 us
    convert_element_type x1, other arithmetic, shards(): (restored.astype(F32) * blend.astype(F32)[:, None] / BLEND).astype(BF16)  1.9 us
    reshape x1, local copies, waits for them, and re-layouts, shards(): hilbert_pos.reshape(1, rows)  1.24 us

profile of v1, /device:TPU:0, one launch (start us, length us, event | category | flops | bytes accessed | tf_op | source)
XLA Modules:
  0.0 60.9 jit_solution(3296660053858884151)
XLA Ops:
  0.0 1.2 %reshape.4.pos = s32[1,384]{1,0:T(1,128)} reshape(s32[384]{0:T(512)} %param.11) | data formatting | bytes 3072 | tf_op jit(solution)/shard_map/reshape | solution.py:296
  1.2 0.0 copy-start
  1.2 57.8 %shard_map.73 = bf16[384,512]{1,0:T(8,128)(2,1)} custom-call(bf16[384,512]{1,0:T(8,128)(2,1)} %tok.1, s32[1,384]{1,0:T(1,128)} %reshape.4.pos, s32[3,8]{1,0:T(4,128)} %listed.1, bf16[1024,512]{1,0:T(8,128)(2,1)} %wq.1, bf16[1024,512]{1,0:T(8,128)(2,1)} %wk.1, bf16[1024,512]{1,0:T(8,128)(2,1)} %wv.1), custom_call_target="tpu_custom_call" | custom-call | tf_op jit(solution)/shard_map/pallas_call | solution.py:258
  59.0 0.0 copy-done
  59.0 1.9 %multiply_convert_fusion = bf16[384,512]{1,0:T(8,128)(2,1)} fusion(bf16[384,512]{1,0:T(8,128)(2,1)} %shard_map.73, f32[384]{0:T(512)S(1)} %convert_element_type.10), kind=kLoop, calls=%fused_computation | loop fusion | flops 786432 | bytes 787968 | tf_op jit(solution)/shard_map/convert_element_type | solution.py:297
  (1 shorter events, 0.0 us)
Async XLA Ops:
  1.2 57.8 %copy-start = (s32[384]{0:T(512)S(1)}, s32[384]{0:T(512)}, u32[]{:S(2)}) copy-start(s32[384]{0:T(512)} %param.13) | copy-start | bytes 4612

commit v2 on v1

--- a/solution.py
+++ b/solution.py
@@ -12,7 +12,8 @@
 REACH = 2
 BLEND = 8
 HEAD_DIM = 64
-PIECES = 2
+PIECES = 4
+PARTS_IN = 2
 WINDOW = 2 * REACH + 1
 LOG2_E = 1.4426950408889634
 MESH = pl.DeviceIdType.MESH
@@ -48,12 +49,13 @@
 
 
 def kernel(
-    n, tok, pos, listed, wq, wk, wv, out,
-    send, recv, code_out, code_in, spread, gather, win, qb, kb, vb, att, back_out, back_in, wq_v, wk_v, wv_v,
+    n, tok, pos, blend, listed, wq, wk, wv, out,
+    send, recv, code_out, code_in, spread, gather, scale, win, qb, kb, vb, att, back_out, back_in, wq_v, wk_v, wv_v,
     w_sem, tok_s, tok_r, code_s, code_r, own_s, fwd_s, win_r, core_s, core_r, back_s, back_r,
 ):
     rows, width = tok.shape
-    pp = send.shape[1]
+    pp = send.shape[2]
+    piece_in = width // PARTS_IN
     per_peer = rows // n
     nb = rows // BLOCK
     total_rows = n * pp
@@ -76,10 +78,14 @@
     for load in loads:
         load.start()
 
-    place = pos[...].astype(F32)
-    column = jnp.sum(
-        jnp.where(iota((rows, rows), 0) == iota((rows, rows), 1), place, 0.0), axis=1, keepdims=True
-    )
+    place = pos[...].reshape(1, rows).astype(F32)
+    diagonal = iota((rows, rows), 0) == iota((rows, rows), 1)
+
+    def stand(row):
+        return jnp.sum(jnp.where(diagonal, row, 0.0), axis=1, keepdims=True)
+
+    column = stand(place)
+    scale[...] = stand(blend[...].reshape(1, rows).astype(F32))
     rank = jnp.sum(jnp.where(column < place, 1.0, 0.0), axis=0, keepdims=True)
     owner = jnp.sum(
         jnp.where(place >= (iota((n, rows), 0) + 1.0) * rows, 1.0, 0.0), axis=0, keepdims=True
@@ -98,36 +104,36 @@
     )
     for d in range(n):
         code_out[d] = codes[d : d + 1, :]
-    send[...] = contract(spread[...], tok[...], 1, 0).astype(BF16).reshape(n, pp, width)
+    for f in range(PARTS_IN):
+        send[f] = (
+            contract(spread[...], tok[:, pl.ds(f * piece_in, piece_in)], 1, 0)
+            .astype(BF16)
+            .reshape(n, pp, piece_in)
+        )
 
     pl.semaphore_wait(barrier, n)
 
     def send_code(k):
         remote(code_out.at[peer(k)], code_in.at[me], code_s.at[k], code_r.at[k], {"blk": peer(k)}).start()
 
-    def send_rows(k):
-        remote(send.at[peer(k)], recv.at[me], tok_s.at[k], tok_r.at[k], {"blk": peer(k)}).start()
+    def rows_copy(f, k, source):
+        return remote(send.at[f, peer(k)], recv.at[f, source], tok_s.at[f, k], tok_r.at[f, k], {"blk": peer(k)})
 
     over_peers(n, send_code)
-    over_peers(n, send_rows)
+    for f in range(PARTS_IN):
+        over_peers(n, lambda k: rows_copy(f, k, me).start())
+        recv[f, me] = send[f, me]
     code_in[me] = code_out[me]
-    recv[me] = send[me]
 
     def take_code(k):
         remote(code_out.at[peer(k)], code_in.at[peer(-k)], code_s.at[k], code_r.at[k], {"blk": peer(k)}).wait()
-
-    def take_rows(k):
-        remote(send.at[peer(k)], recv.at[peer(-k)], tok_s.at[k], tok_r.at[k], {"blk": peer(k)}).wait()
 
     over_peers(n, take_code)
     arrived = jnp.sum(code_in[...], axis=0)
     gather[...] = jnp.where(iota((rows, total_rows), 0) + 1.0 == arrived, 1.0, 0.0).astype(BF16)
-    over_peers(n, take_rows)
-    placed = contract(gather[...], recv[...].reshape(total_rows, width), 1, 0).astype(BF16)
-    win[half, REACH] = placed
 
     def piece(step, c):
-        return win.at[half, REACH + step, pl.ds(c * BLOCK, BLOCK)]
+        return win.at[half * PARTS_IN + c, REACH + step]
 
     def own_copy(i, step, c):
         return remote(
@@ -148,30 +154,35 @@
     def core_arrival(step, c):
         return remote(
             piece(step, c),
-            win.at[1 - half, REACH + step, pl.ds(c * BLOCK, BLOCK)],
+            win.at[(1 - half) * PARTS_IN + c, REACH + step],
             core_s.at[REACH + step, c],
             core_r.at[REACH + step, c],
             other,
         )
 
     steps_out = (-2 * e, 2 * e, e)
-    for c in range(nb):
-        for i, step in enumerate(steps_out):
-            own_copy(i, step, c).start()
+    for c in range(PARTS_IN):
+        over_peers(n, lambda k: rows_copy(c, k, peer(-k)).wait())
+        win[half * PARTS_IN + c, REACH] = contract(
+            gather[...], recv[c].reshape(total_rows, piece_in), 1, 0
+        ).astype(BF16)
+        own_copy(0, steps_out[0], c).start()
         core_copy(0, c).start()
+        for i in (1, 2):
+            own_copy(i, steps_out[i], c).start()
 
     def project(step, with_query):
-        for c in range(nb):
+        for c in range(PARTS_IN):
             core_arrival(step, c).wait_recv()
         slot = REACH + step
-        whole = jnp.concatenate([win[0, slot], win[1, slot]], axis=1)
+        whole = jnp.concatenate([win[g, slot] for g in range(2 * PARTS_IN)], axis=1)
         if with_query:
             qb[...] = contract(whole, wq_v[...], 1, 0).astype(BF16).reshape(nb, BLOCK, width)
         kb[pl.ds(slot * nb, nb)] = contract(whole, wk_v[...], 1, 0).astype(BF16).reshape(nb, BLOCK, width)
         vb[pl.ds(slot * nb, nb)] = contract(whole, wv_v[...], 1, 0).astype(BF16).reshape(nb, BLOCK, width)
 
     def pass_on(step, forward):
-        for c in range(nb):
+        for c in range(PARTS_IN):
             arrival(step, c).wait_recv()
             if forward:
                 fwd_copy(c).start()
@@ -220,9 +231,7 @@
 
     for f in range(PIECES):
         for p in range(pairs):
-
-            @pl.loop(0, nb)
-            def _(b):
+            for b in range(nb):
                 att[b, :, pl.ds(p * 2 * HEAD_DIM, 2 * HEAD_DIM)] = attend(b, p, f * part + p * 2 * HEAD_DIM)
 
         back_out[f] = (
@@ -231,7 +240,7 @@
         over_peers(n, lambda k: back_copy(f, k, me).start())
         back_in[f, me] = back_out[f, me]
 
-    for c in range(nb):
+    for c in range(PARTS_IN):
         for i, step in enumerate(steps_out):
             own_copy(i, step, c).wait_send()
         fwd_copy(c).wait_send()
@@ -240,9 +249,8 @@
 
     for f in range(PIECES):
         over_peers(n, lambda k: back_copy(f, k, peer(-k)).wait())
-        out[:, pl.ds(f * part, part)] = contract(
-            spread[...], back_in[f].reshape(total_rows, part), 0, 0
-        ).astype(BF16)
+        restored = contract(spread[...], back_in[f].reshape(total_rows, part), 0, 0)
+        out[:, pl.ds(f * part, part)] = (restored * scale[...] * (1.0 / BLEND)).astype(BF16)
 
 
 def shards(n, tokens, w_query, w_key, w_value, hilbert_pos, key_blocks, blend):
@@ -255,19 +263,20 @@
     vmem = pl.BlockSpec(memory_space=pltpu.VMEM)
     anywhere = pl.BlockSpec(memory_space=pl.ANY)
     dma = pltpu.SemaphoreType.DMA
-    restored = pl.pallas_call(
+    return pl.pallas_call(
         functools.partial(kernel, n),
         out_shape=jax.ShapeDtypeStruct((rows, width), BF16),
-        in_specs=[vmem, vmem, pl.BlockSpec(memory_space=pltpu.SMEM), anywhere, anywhere, anywhere],
+        in_specs=[vmem, vmem, vmem, pl.BlockSpec(memory_space=pltpu.SMEM), anywhere, anywhere, anywhere],
         out_specs=vmem,
         scratch_shapes=[
-            pltpu.VMEM((n, pp, width), BF16),
-            pltpu.VMEM((n, pp, width), BF16),
+            pltpu.VMEM((PARTS_IN, n, pp, width // PARTS_IN), BF16),
+            pltpu.VMEM((PARTS_IN, n, pp, width // PARTS_IN), BF16),
             pltpu.VMEM((n, 1, n * pp), F32),
             pltpu.VMEM((n, 1, n * pp), F32),
             pltpu.VMEM((n * pp, rows), BF16),
             pltpu.VMEM((rows, n * pp), BF16),
-            pltpu.VMEM((2, WINDOW, rows, width), BF16),
+            pltpu.VMEM((rows, 1), F32),
+            pltpu.VMEM((2 * PARTS_IN, WINDOW, rows, width // PARTS_IN), BF16),
             pltpu.VMEM((nb, BLOCK, width), BF16),
             pltpu.VMEM((WINDOW * nb, BLOCK, width), BF16),
             pltpu.VMEM((WINDOW * nb, BLOCK, width), BF16),
@@ -278,23 +287,22 @@
             pltpu.VMEM((depth, width), BF16),
             pltpu.VMEM((depth, width), BF16),
             dma((3,)),
+            dma((PARTS_IN, n)),
+            dma((PARTS_IN, n)),
             dma((n,)),
             dma((n,)),
-            dma((n,)),
-            dma((n,)),
-            dma((3, nb)),
-            dma((nb,)),
-            dma((WINDOW, nb)),
-            dma((WINDOW, nb)),
-            dma((WINDOW, nb)),
+            dma((3, PARTS_IN)),
+            dma((PARTS_IN,)),
+            dma((WINDOW, PARTS_IN)),
+            dma((WINDOW, PARTS_IN)),
+            dma((WINDOW, PARTS_IN)),
             dma((PIECES, n)),
             dma((PIECES, n)),
         ],
         compiler_params=pltpu.CompilerParams(
             collective_id=0, has_side_effects=True, vmem_limit_bytes=56 * 1024 * 1024
         ),
-    )(tokens, hilbert_pos.reshape(1, rows), key_blocks, w_query, w_key, w_value)
-    return (restored.astype(F32) * blend.astype(F32)[:, None] / BLEND).astype(BF16)
+    )(tokens, hilbert_pos, blend, key_blocks, w_query, w_key, w_value)
 
 
 def solution(mesh):

time: 61.1 us -> 56 us (0.917)
  Pallas kernels: 57.8 us -> 54.1 us
  other arithmetic: 1.91 us -> 0 us
    pallas_call x1, Pallas kernels: 57.8 us -> 54.1 us  [shards(): pl.pallas_call(functools.partial(kernel, n), out_shape=jax.ShapeDtypeStru...]
    convert_element_type x2 -> x0, other arithmetic: 1.91 us -> none  [the longest x1 1.9 us: shards(): (restored.astype(F32) * blend.astype(F32)[:, None] / BLEND).astype(BF16)]
    unnamed x2 -> x1, local copies, waits for them, and re-layouts: 0.01 us -> 1.77 us
    reshape x1 -> x0, local copies, waits for them, and re-layouts: 1.24 us -> none  [shards(): hilbert_pos.reshape(1, rows)]
where the time goes in v2:
time: 56 us; the launch traced here: 55.9 us
  Pallas kernels  54.1 us (97%)
  local copies, waits for them, and re-layouts  1.77 us (3%)
    pallas_call x1, Pallas kernels, shards(): pl.pallas_call(functools.partial(kernel, n), out_shape=jax.ShapeDtypeStru...  54.1 us
    unnamed x1, local copies, waits for them, and re-layouts  1.77 us

profile of v2, /device:TPU:0, one launch (start us, length us, event | category | flops | bytes accessed | tf_op | source)
XLA Modules:
  0.0 55.9 jit_solution(4092555806986923617)
XLA Ops:
  0.0 54.1 %shard_map.73 = bf16[384,512]{1,0:T(8,128)(2,1)} custom-call(bf16[384,512]{1,0:T(8,128)(2,1)} %tok.1, s32[384]{0:T(512)} %pos.1, s32[384]{0:T(512)} %blend.1, s32[3,8]{1,0:T(4,128)} %listed.1, bf16[1024,512]{1,0:T(8,128)(2,1)} %wq.1, bf16[1024,512]{1,0:T(8,128)(2,1)} %wk.1, bf16[1024,512]{1,0:T(8,128)(2,1)} %wv.1), custom_call_target="tpu_custom_call" | custom-call | tf_op jit(solution)/shard_map/pallas_call | solution.py:266
  54.1 1.8 %copy.9 = bf16[384,512]{1,0:T(8,128)(2,1)} copy(bf16[384,512]{1,0:T(8,128)(2,1)} %shard_map.73) | data formatting | bytes 786432

commit v3 on v2

--- a/solution.py
+++ b/solution.py
@@ -196,8 +196,8 @@
     project(2 * e, False)
     project(e, False)
     pass_on(-2 * e, False)
+    pass_on(-e, False)
     project(-2 * e, False)
-    pass_on(-e, False)
     project(-e, False)
 
     first = lax.broadcasted_iota(jnp.int32, (BLOCK, 2 * HEAD_DIM), 1) < HEAD_DIM

time: 56 us -> 56.5 us (level)
  no operation moved by 1% of the time
where the time goes in v3:
time: 56.5 us; the launch traced here: 56.3 us
  Pallas kernels  54.6 us (97%)
  local copies, waits for them, and re-layouts  1.77 us (3%)
    pallas_call x1, Pallas kernels, shards(): pl.pallas_call(functools.partial(kernel, n), out_shape=jax.ShapeDtypeStru...  54.6 us
    unnamed x1, local copies, waits for them, and re-layouts  1.77 us

profile of v3, /device:TPU:0, one launch (start us, length us, event | category | flops | bytes accessed | tf_op | source)
XLA Modules:
  0.0 56.3 jit_solution(403466328236341300)
XLA Ops:
  0.0 54.6 %shard_map.73 = bf16[384,512]{1,0:T(8,128)(2,1)} custom-call(bf16[384,512]{1,0:T(8,128)(2,1)} %tok.1, s32[384]{0:T(512)} %pos.1, s32[384]{0:T(512)} %blend.1, s32[3,8]{1,0:T(4,128)} %listed.1, bf16[1024,512]{1,0:T(8,128)(2,1)} %wq.1, bf16[1024,512]{1,0:T(8,128)(2,1)} %wk.1, bf16[1024,512]{1,0:T(8,128)(2,1)} %wv.1), custom_call_target="tpu_custom_call" | custom-call | tf_op jit(solution)/shard_map/pallas_call | solution.py:266
  54.6 1.8 %copy.9 = bf16[384,512]{1,0:T(8,128)(2,1)} copy(bf16[384,512]{1,0:T(8,128)(2,1)} %shard_map.73) | data formatting | bytes 786432
